TPU v7x, 32 devices: a whole 2x2x4 slice. The times are simulated.
32 devices in a mesh: space: 8 (over z, x), scal: 4 (over y, core).
Axes of the slice: x: 2, y: 2, z: 4, core: 2. Of those that a mesh axis runs over, the one named last changes fastest.
Arguments:
- scalars: float32 [128, 512, 256], P('scal', 'space'), may hold values from -6 to 6
- schmidt: float32 [128], P('scal'), may hold values from 1 to 1000
- velocity_history: bfloat16 [8, 2, 64, 256], P('scal', None, 'space'), may hold values from -0.796875 to 0.796875
- fine_src: int32 [512], replicated, may hold values from 0 to 62, as said below
- remap_weight: float32 [512], replicated, may hold values from 0 to 1
- snap_step: int32 [2], replicated, may hold values from 0 to 7
Outputs:
- transported: float32 [128, 512, 256], P('scal', 'space')
Inputs may be any that keep to these rules, and one draw needn't show every extreme that they name: fine_src may name any coarse row of any tile, in no particular order.
All inputs are finite; a program needn't handle non-finite values.
Results may differ from a plain program's by a relative error of at most 0.0003.
Values may be sent and summed in bfloat16 or wider, within the bound.
A program may use at most 64 MiB of HBM per device.

v0:
```python
import jax
import jax.numpy as jnp
from jax import lax
from jax.sharding import PartitionSpec as P

STEPS = 2


diffusion_scale = 0.24


def from_root(value, axis, source):
    kept = jnp.where(lax.axis_index(axis) == source, value, 0).astype(value.dtype)
    return lax.psum(kept, axis)


def padded_2(cells, sides, width):
    for axis, dim in sides:
        count = lax.axis_size(axis)
        ends = count - 1
        head = lax.slice_in_dim(cells, 0, width, axis=dim)
        tail = lax.slice_in_dim(cells, cells.shape[dim] - width, cells.shape[dim], axis=dim)
        cells = jnp.concatenate(
            [
                lax.ppermute(tail, axis, [(i, (i + 1) % count) for i in range(ends)]),
                cells,
                lax.ppermute(head, axis, [((i + 1) % count, i) for i in range(ends)]),
            ],
            axis=dim,
        )
    return cells


def advance(padded, velocity, diffusivity):
    center = padded[:, 1:-1]
    upper_row = padded[:, 2:]
    lower_row = padded[:, :-2]
    east_cell = jnp.roll(center, -1, axis=2)
    west_cell = jnp.roll(center, 1, axis=2)
    laplacian = upper_row + lower_row + east_cell + west_cell - 4.0 * center
    return (
        center
        - velocity[0] * (0.5 * (upper_row - lower_row))
        - velocity[1] * (0.5 * (east_cell - west_cell))
        + diffusivity[:, None, None] * laplacian
    )


def body(scalars, schmidt, velocity_history, fine_src, remap_weight, snap_step):
    tile_rows = scalars.shape[1]
    snap_dev = velocity_history.shape[0]
    coarse_dev = velocity_history.shape[2]
    tile_count = lax.axis_size("space")
    coarse_total = coarse_dev * tile_count
    anchor = lax.axis_index("space") * tile_rows
    diffusivity = diffusion_scale / schmidt
    padded_src = jnp.pad(fine_src, (1, 1))
    padded_weight = jnp.pad(remap_weight, (1, 1))
    field = scalars
    for step_index in range(STEPS):
        padded = padded_2(field, (("space", 1),), 1)
        row_count = tile_rows + 2 * 0
        source_rows = lax.dynamic_slice_in_dim(padded_src, anchor + 1 - 0, row_count)
        weights = lax.dynamic_slice_in_dim(padded_weight, anchor + 1 - 0, row_count)
        coarse_index = lax.broadcasted_iota(jnp.int32, (row_count, coarse_total), 1)
        selection = jnp.where(
            coarse_index == source_rows[:, None], (1.0 - weights)[:, None], 0.0
        ) + jnp.where(coarse_index == source_rows[:, None] + 1, weights[:, None], 0.0)
        snapshot = snap_step[step_index]
        owner_index = snapshot // snap_dev
        own_slot = lax.dynamic_index_in_dim(
            velocity_history, snapshot % snap_dev, 0, keepdims=False
        )
        fine_velocity = jnp.einsum(
            "rn,cnz->crz",
            selection,
            lax.all_gather(own_slot, "space", axis=1, tiled=True).astype(jnp.float32),
            precision=lax.Precision.HIGHEST,
        )
        result_velocity = from_root(fine_velocity, "scal", owner_index)
        field = advance(padded, result_velocity, diffusivity)
    return field


def solution(mesh):
    return jax.shard_map(
        body,
        mesh=mesh,
        in_specs=(
            P("scal", "space", None),
            P("scal"),
            P("scal", None, "space", None),
            P(),
            P(),
            P(),
        ),
        out_specs=P("scal", "space", None),
        check_vma=False,
    )
```

profile of v0, /device:TPU:0, one launch (start us, length us, event | category | flops | bytes accessed | tf_op | source)
XLA Modules:
  0.0 145.1 jit_solution(16891789043258557029)
XLA Ops:
  6.5 1.1 fusion.25
  7.6 4.8 %collective-permute-start.1 = (f32[32,1,256]{2,1,0:T(1,128)S(1)}, f32[32,1,256]{2,1,0:T(1,128)S(1)}, u32[]{:S(2)}, u32[]{:S(2)}) collective-permute-start(f32[32,1,256]{2,1,0:T(1,128)S(1)} %get-tuple-element.17), channel_id=1, source_target_pairs={{0,4},{4,8},{8,12},{12,16},{16,20},{20,24},{24,28},{1,5},{5,9},{9,... | collective-permute-start | bytes 98312 | tf_op jit(solution)/shard_map/ppermute | solution.py:25
  12.5 1.3 collective-permute-start
  13.8 1.3 fusion.28
  20.2 0.8 broadcast_add_fusion
  21.0 0.8 broadcast_subtract_fusion
  21.7 0.8 constant_dynamic-slice_fusion
  22.5 32.9 %all-gather.1 = bf16[1,2,64,256]{3,2,1,0:T(8,128)(2,1)S(1)} all-gather(bf16[1,2,8,256]{3,2,1,0:T(8,128)(2,1)S(1)} %get-tuple-element.27), channel_id=3, replica_groups=mesh['space'=8,'scal'=4] {'space'}, dimensions={2}, use_global_device_ids=true | all-gather | bytes 73728 | tf_op jit(solution)/shard_map/all_gather | solution.py:77
  55.4 30.5 %all-gather = bf16[1,2,64,256]{3,2,1,0:T(8,128)(2,1)S(1)} all-gather(bf16[1,2,8,256]{3,2,1,0:T(8,128)(2,1)S(1)} %get-tuple-element.28), channel_id=2, replica_groups=mesh['space'=8,'scal'=4] {'space'}, dimensions={2}, use_global_device_ids=true | all-gather | bytes 73728 | tf_op jit(solution)/shard_map/all_gather | solution.py:77
  85.9 0.9 fusion
  86.8 0.9 fusion.1
  87.7 0.0 all-reduce.5.cloned.1.call-update
  87.8 3.0 %fusion.27 = (f32[32,64,1]{2,1,0:T(8,128)S(1)}, f32[32,64,1]{2,1,0:T(8,128)}) fusion(f32[32,64,256]{2,1,0:T(8,128)} %param.6), kind=kLoop, calls=%fused_computation.53 | loop fusion | bytes 32768 | tf_op jit(solution)/shard_map/jit(_roll_static)/slice | solution.py:38
  90.8 2.8 %fusion.26 = (f32[32,64,255]{2,1,0:T(8,128)}, f32[32,64,255]{2,1,0:T(8,128)}) fusion(f32[32,64,256]{2,1,0:T(8,128)S(1)} %copy-done), kind=kLoop, calls=%fused_computation.52 | loop fusion | bytes 8355840 | tf_op jit(solution)/shard_map/jit(_roll_static)/slice | solution.py:38
  93.6 26.4 %all-reduce.5.cloned.1.call-done = (f32[2,64,256]{2,1,0:T(8,128)}, f32[2,64,256]{2,1,0:T(8,128)}) async-done(((f32[2,64,256]{2,1,0:T(8,128)}, f32[2,64,256]{2,1,0:T(8,128)}), (f32[2,64,256]{2,1,0:T(8,128)}, f32[2,64,256]{2,1,0:T(8,128)})) %all-reduce.5.cloned.1.call-update) | async-done | bytes 262160 | tf_op jit(solution)/shard_map/psum | solution.py:14
  120.0 0.9 fusion.5
  120.9 3.8 %multiply_add_fusion.1 = f32[32,64,256]{2,1,0:T(8,128)S(1)} fusion(f32[32,64,256]{2,1,0:T(8,128)S(1)} %copy-done, f32[32,64,255]{2,1,0:T(8,128)} %get-tuple-element.20, f32[32,64,1]{2,1,0:T(8,128)} %get-tuple-element.22, f32[32,64,1]{2,1,0:T(8,128)S(1)} %get-tuple-element.21, f32[32,64,255]{2,1,0:T(8,128)} %get-tuple-element.19, ...), kind=kLoop, calls=%fused_computation.9 | loop fusion | flops 8912896 | bytes 8585344 | tf_op jit(solution)/shard_map/add | solution.py:42
  124.8 0.4 fusion.24
  125.2 0.7 fusion.23
  126.0 3.4 %collective-permute-start.3 = (f32[32,1,256]{2,1,0:T(1,128)S(1)}, f32[32,1,256]{2,1,0:T(1,128)S(1)}, u32[]{:S(2)}, u32[]{:S(2)}) collective-permute-start(f32[32,1,256]{2,1,0:T(1,128)S(1)} %get-tuple-element.11), channel_id=1, source_target_pairs={{0,4},{4,8},{8,12},{12,16},{16,20},{20,24},{24,28},{1,5},{5,9},{9,... | collective-permute-start | bytes 98312 | tf_op jit(solution)/shard_map/ppermute | solution.py:25
  129.3 1.3 collective-permute-start.2
  130.7 0.2 collective-permute-done.3
  130.9 4.2 %collective-permute-done.2 = f32[32,1,256]{2,1,0:T(1,128)S(1)} collective-permute-done((f32[32,1,256]{2,1,0:T(1,128)S(1)}, f32[32,1,256]{2,1,0:T(1,128)S(1)}, u32[]{:S(2)}, u32[]{:S(2)}) %collective-permute-start.2) | collective-permute-done | bytes 32800 | tf_op jit(solution)/shard_map/ppermute | solution.py:27
  135.1 3.1 %multiply_add_fusion = f32[32,64,256]{2,1,0:T(8,128)} fusion(f32[32,64,256]{2,1,0:T(8,128)S(1)} %multiply_add_fusion.1, f32[32,64,255]{2,1,0:T(8,128)S(1)} %get-tuple-element.14, f32[32,64,1]{2,1,0:T(8,128)S(1)} %get-tuple-element.16, f32[32,64,1]{2,1,0:T(8,128)S(1)} %get-tuple-element.15, f32[32,64,255]{2,1,0:T(8,128)S(1)} %get-tuple-element.13, ...), kind=kLoop, calls=%fused_computation.8 | loop fusion | flops 8912896 | bytes 8585344 | tf_op jit(solution)/shard_map/add | solution.py:42
  (12 shorter events, 0.1 us)
Async XLA Ops:
  6.5 113.5 %all-reduce.5.cloned.1.call-start = ((), (), s32[]{:S(2)}) async-start(), calls=%async_computation | async-start | bytes 524288 | tf_op jit(solution)/shard_map/psum | solution.py:14
  7.6 113.3 %collective-permute-start.1 = (f32[32,1,256]{2,1,0:T(1,128)S(1)}, f32[32,1,256]{2,1,0:T(1,128)S(1)}, u32[]{:S(2)}, u32[]{:S(2)}) collective-permute-start(f32[32,1,256]{2,1,0:T(1,128)S(1)} %get-tuple-element.17), channel_id=1, source_target_pairs={{0,4},{4,8},{8,12},{12,16},{16,20},{20,24},{24,28},{1,5},{5,9},{9,... | collective-permute-start | bytes 98312 | tf_op jit(solution)/shard_map/ppermute | solution.py:25
  12.5 108.4 %collective-permute-start = (f32[32,1,256]{2,1,0:T(1,128)S(1)}, f32[32,1,256]{2,1,0:T(1,128)S(1)}, u32[]{:S(2)}, u32[]{:S(2)}) collective-permute-start(f32[32,1,256]{2,1,0:T(1,128)S(1)} %get-tuple-element.18), channel_id=1, source_target_pairs={{4,0},{8,4},{12,8},{16,12},{20,16},{24,20},{28,24},{5,1},{9,5},{13... | collective-permute-start | bytes 98312 | tf_op jit(solution)/shard_map/ppermute | solution.py:27
  87.8 3.1 %copy-start = (f32[32,64,256]{2,1,0:T(8,128)S(1)}, f32[32,64,256]{2,1,0:T(8,128)}, u32[]{:S(2)}) copy-start(f32[32,64,256]{2,1,0:T(8,128)} %param.6) | copy-start | bytes 6291460
  90.8 2.8 %copy-start.2 = (f32[32]{0:T(128)S(1)}, f32[32]{0:T(128)}, u32[]{:S(2)}) copy-start(f32[32]{0:T(128)} %param.7) | copy-start | bytes 388
  125.2 5.4 %copy-start.1 = (f32[2,64,256]{2,1,0:T(8,128)S(1)}, f32[2,64,256]{2,1,0:T(8,128)}, u32[]{:S(2)}) copy-start(f32[2,64,256]{2,1,0:T(8,128)} %get-tuple-element.6) | copy-start | bytes 393220
  126.0 5.0 %collective-permute-start.3 = (f32[32,1,256]{2,1,0:T(1,128)S(1)}, f32[32,1,256]{2,1,0:T(1,128)S(1)}, u32[]{:S(2)}, u32[]{:S(2)}) collective-permute-start(f32[32,1,256]{2,1,0:T(1,128)S(1)} %get-tuple-element.11), channel_id=1, source_target_pairs={{0,4},{4,8},{8,12},{12,16},{16,20},{20,24},{24,28},{1,5},{5,9},{9,... | collective-permute-start | bytes 98312 | tf_op jit(solution)/shard_map/ppermute | solution.py:25
  129.3 5.8 %collective-permute-start.2 = (f32[32,1,256]{2,1,0:T(1,128)S(1)}, f32[32,1,256]{2,1,0:T(1,128)S(1)}, u32[]{:S(2)}, u32[]{:S(2)}) collective-permute-start(f32[32,1,256]{2,1,0:T(1,128)S(1)} %get-tuple-element.12), channel_id=1, source_target_pairs={{4,0},{8,4},{12,8},{16,12},{20,16},{24,20},{28,24},{5,1},{9,5},{13... | collective-permute-start | bytes 98312 | tf_op jit(solution)/shard_map/ppermute | solution.py:27
Sparse Core Ops, SparseCore 0:
  87.9 32.0 all-reduce.4
where the time goes:
time: 146 us; the launch traced here: 145 us
  blocking collectives  63.4 us (43%)
  waiting for transfers between devices  30.9 us (21%)
  between operations  18.7 us (13%)
  starting transfers between devices  10.8 us (7%)
  local copies, waits for them, and re-layouts  10.2 us (7%)
  other arithmetic  9.39 us (6%)
  matrix products  1.83 us (1%)
    all_gather x2, blocking collectives, body(): lax.all_gather(own_slot, 'space', axis=1, tiled=True).astype(jnp.float32)  63.4 us
    psum x1, waiting for transfers between devices, from_root(): return lax.psum(kept, axis)  26.4 us
    ppermute x2, starting transfers between devices, padded_2(): lax.ppermute(tail, axis, [(i, (i + 1) % count) for i in range(ends)])  8.22 us
    add x2, other arithmetic, advance(): center - velocity[0] * (0.5 * (upper_row - lower_row))  6.97 us
    slice x4, local copies, waits for them, and re-layouts, advance(): east_cell = jnp.roll(center, -1, axis=2)  6.96 us
    ppermute x2, waiting for transfers between devices, padded_2(): lax.ppermute(head, axis, [((i + 1) % count, i) for i in range(ends)])  4.23 us
  transfers between devices with their start and end apart: 5, of which 3 were waited for; matrix products, arithmetic and copies ran while one was open for 8% of the time, Pallas kernels for 0%

commit v1 on v0

v1 whole, which is shorter than its diff:
```python
import functools

import jax
import jax.numpy as jnp
from jax import lax
from jax.experimental import pallas as pl
from jax.experimental.pallas import tpu as pltpu
from jax.sharding import PartitionSpec as P

MESH = pl.DeviceIdType.MESH
LANES = 128
GROUPS = 4


def gather_kernel(
    n_space, n_scal, snap, src, wgt, hist, field, halo, vel,
    mine, part, coarse, select, halo_send, halo_recv, part_send, part_recv,
    row_send, row_recv,
):
    tile = lax.axis_index("space")
    group = lax.axis_index("scal")
    slots, comps, depth, width = hist.shape
    steps = vel.shape[0]
    rows = field.shape[1]
    ring = rows + 8
    last = n_space - 1

    barrier = pltpu.get_barrier_semaphore()
    halo[...] = jnp.zeros_like(halo)
    for o in range(1, n_scal):
        pl.semaphore_signal(
            barrier, inc=1, device_id=(tile, lax.rem(group + o, n_scal)), device_id_type=MESH
        )
    for o in range(1, n_space):
        pl.semaphore_signal(
            barrier, inc=1, device_id=(lax.rem(tile + o, n_space), group), device_id_type=MESH
        )

    for t in range(steps):
        wanted = jnp.full((comps * depth, width), snap[t], jnp.int32)
        kept = jnp.zeros((comps * depth, width), jnp.float32)
        for k in range(slots):
            rows_k = hist[k].reshape(comps * depth, width).astype(jnp.float32)
            kept = jnp.where(wanted == group * slots + k, rows_k, kept)
        mine[t] = kept.astype(mine.dtype)

    pl.semaphore_wait(barrier, n_scal - 1 + n_space - 1)

    part_copies = []
    for o in range(1, n_scal):
        copy = pltpu.make_async_remote_copy(
            src_ref=mine, dst_ref=part.at[o], send_sem=part_send.at[o], recv_sem=part_recv.at[o],
            device_id=(tile, lax.rem(group + o, n_scal)), device_id_type=MESH,
        )
        copy.start()
        part_copies.append(copy)

    above = pltpu.make_async_remote_copy(
        src_ref=field.at[:, pl.ds(rows - 2, 2), :], dst_ref=halo.at[:, pl.ds(6, 2), :],
        send_sem=halo_send.at[0], recv_sem=halo_recv.at[0],
        device_id=(lax.rem(tile + 1, n_space), group), device_id_type=MESH,
    )
    below = pltpu.make_async_remote_copy(
        src_ref=field.at[:, pl.ds(0, 2), :], dst_ref=halo.at[:, pl.ds(0, 2), :],
        send_sem=halo_send.at[1], recv_sem=halo_recv.at[1],
        device_id=(lax.rem(tile + last, n_space), group), device_id_type=MESH,
    )

    @pl.when(tile < last)
    def _():
        above.start()

    @pl.when(tile > 0)
    def _():
        below.start()

    def window(ref):
        whole = jnp.broadcast_to(ref[...], (8, ref.shape[1]))
        total = whole.shape[1]
        turned = pltpu.roll(whole, lax.rem(total - tile * rows, total), 1)
        lane = lax.broadcasted_iota(jnp.int32, (8, LANES), 1)
        tail = pltpu.roll(turned[:, total - LANES :], ring % LANES, 1)
        return jnp.where(lane == ring - 1, tail, turned[:, :LANES])[:1]

    source, weight = window(src), window(wgt)
    index = lax.broadcasted_iota(jnp.int32, (n_space * comps * depth, LANES), 0)
    row = index // (comps * depth) * depth + index % depth
    comp = index // depth % comps
    value = jnp.where(row == source, 0.5 * (1.0 - weight), 0.0) + jnp.where(
        row == source + 1, 0.5 * weight, 0.0
    )
    first = value.astype(jnp.bfloat16).astype(jnp.float32)
    second = (value - first).astype(jnp.bfloat16).astype(jnp.float32)
    third = value - first - second
    for c in range(comps):
        for k, term in enumerate((first, second, third)):
            chosen = jnp.where(comp == c, term, 0.0).T
            select[pl.ds((c * 3 + k) * LANES, LANES), :] = chosen.astype(select.dtype)

    for copy in part_copies:
        copy.wait_recv()
    total = mine[...].astype(jnp.float32)
    for o in range(1, n_scal):
        total = total + part[o].astype(jnp.float32)
    own = pl.ds(pl.multiple_of(tile * (comps * depth), comps * depth), comps * depth)
    coarse[:, own, :] = total.astype(coarse.dtype)
    row_copies = []
    for o in range(1, n_space):
        copy = pltpu.make_async_remote_copy(
            src_ref=coarse.at[:, own, :], dst_ref=coarse.at[:, own, :],
            send_sem=row_send.at[o], recv_sem=row_recv.at[o],
            device_id=(lax.rem(tile + o, n_space), group), device_id_type=MESH,
        )
        copy.start()
        row_copies.append(copy)
    for copy in part_copies:
        copy.wait_send()
    for copy in row_copies:
        copy.wait_recv()
    for t in range(steps):
        fine = jnp.dot(select[...], coarse[t], preferred_element_type=jnp.float32)
        for c in range(comps):
            at = [(c * 3 + k) * LANES for k in range(3)]
            vel[t, c] = (fine[at[2] : at[2] + ring] + fine[at[1] : at[1] + ring]) + fine[at[0] : at[0] + ring]
    for copy in row_copies:
        copy.wait_send()

    @pl.when(tile < last)
    def _():
        above.wait_send()
        below.wait_recv()

    @pl.when(tile > 0)
    def _():
        below.wait_send()
        above.wait_recv()


def stencil_kernel(n_space, sch, halo, vel, field, out, held, made, in_sem, out_sem):
    tile = lax.axis_index("space")
    count, rows, width = field.shape
    steps = vel.shape[0]
    each = count // GROUPS
    tiles = rows // 8
    loads = []
    for g in range(GROUPS):
        part = pl.ds(g * each, each)
        loads.append(pltpu.make_async_copy(field.at[part], held.at[part], in_sem.at[g]))
        loads[-1].start()
    sub = lax.broadcasted_iota(jnp.int32, (8, width), 0)
    is_first, is_last = sub == 0, sub == 7
    outside = (is_first & (tile == n_space - 1)) | (is_last & (tile == 0))

    def advance(cells, t, diff, keep, wanted):
        ups = [pltpu.roll(u, 7, 0) for u in cells]
        downs = [pltpu.roll(u, 1, 0) for u in cells]
        n = len(cells)
        result = []
        for j in range(wanted):
            u = cells[j]
            up = jnp.where(is_last, ups[(j + 1) % n], ups[j])
            down = jnp.where(is_first, downs[(j - 1) % n], downs[j])
            east = pltpu.roll(u, width - 1, 1)
            west = pltpu.roll(u, 1, 1)
            at = pl.ds(8 * j, 8)
            result.append(
                keep * u
                + diff * ((up + down) + (east + west))
                - vel[t, 0, at, :] * (up - down)
                - vel[t, 1, at, :] * (east - west)
            )
        return result

    stores = []
    for g in range(GROUPS):
        loads[g].wait()

        def one(i, carry):
            s = g * each + i
            diff = 0.24 / jnp.full((8, LANES), sch[s], jnp.float32)
            diff = jnp.concatenate([diff] * (width // LANES), axis=1)
            keep = 1.0 - 4.0 * diff
            cells = [held[s, pl.ds(8 * j, 8), :] for j in range(tiles)] + [halo[s]]
            for t in range(steps):
                final = t == steps - 1
                cells = advance(cells, t, diff, keep, tiles if final else tiles + 1)
                if not final:
                    cells[-1] = jnp.where(outside, 0.0, cells[-1])
            for j in range(tiles):
                made[s, pl.ds(8 * j, 8), :] = cells[j]
            return carry

        lax.fori_loop(0, each, one, 0)
        part = pl.ds(g * each, each)
        stores.append(pltpu.make_async_copy(made.at[part], out.at[part], out_sem.at[g]))
        stores[-1].start()
    for store in stores:
        store.wait()


def solution(mesh):
    n_space, n_scal = mesh.shape["space"], mesh.shape["scal"]

    def body(scalars, schmidt, velocity_history, fine_src, remap_weight, snap_step):
        count, rows, width = scalars.shape
        _, comps, depth, _ = velocity_history.shape
        steps = snap_step.shape[0]
        vmem = pl.BlockSpec(memory_space=pltpu.VMEM)
        smem = pl.BlockSpec(memory_space=pltpu.SMEM)
        anywhere = pl.BlockSpec(memory_space=pl.ANY)
        own = comps * depth
        halo, vel = pl.pallas_call(
            functools.partial(gather_kernel, n_space, n_scal),
            out_shape=(
                jax.ShapeDtypeStruct((count, 8, width), jnp.float32),
                jax.ShapeDtypeStruct((steps, comps, rows + 8, width), jnp.float32),
            ),
            in_specs=[smem, vmem, vmem, vmem, anywhere],
            out_specs=(vmem, vmem),
            scratch_shapes=[
                pltpu.VMEM((steps, own, width), jnp.bfloat16),
                pltpu.VMEM((n_scal, steps, own, width), jnp.bfloat16),
                pltpu.VMEM((steps, n_space * own, width), jnp.bfloat16),
                pltpu.VMEM((3 * comps * LANES, n_space * own), jnp.bfloat16),
                pltpu.SemaphoreType.DMA((2,)),
                pltpu.SemaphoreType.DMA((2,)),
                pltpu.SemaphoreType.DMA((n_scal,)),
                pltpu.SemaphoreType.DMA((n_scal,)),
                pltpu.SemaphoreType.DMA((n_space,)),
                pltpu.SemaphoreType.DMA((n_space,)),
            ],
            compiler_params=pltpu.CompilerParams(
                collective_id=0, has_side_effects=True, vmem_limit_bytes=16 * 2**20
            ),
        )(snap_step, fine_src[None], remap_weight[None], velocity_history, scalars)
        return pl.pallas_call(
            functools.partial(stencil_kernel, n_space),
            out_shape=jax.ShapeDtypeStruct(scalars.shape, jnp.float32),
            in_specs=[smem, vmem, vmem, anywhere],
            out_specs=anywhere,
            scratch_shapes=[
                pltpu.VMEM(scalars.shape, jnp.float32),
                pltpu.VMEM(scalars.shape, jnp.float32),
                pltpu.SemaphoreType.DMA((GROUPS,)),
                pltpu.SemaphoreType.DMA((GROUPS,)),
            ],
            compiler_params=pltpu.CompilerParams(vmem_limit_bytes=24 * 2**20),
        )(schmidt, halo, vel, scalars)

    return jax.shard_map(
        body,
        mesh=mesh,
        in_specs=(
            P("scal", "space", None),
            P("scal"),
            P("scal", None, "space", None),
            P(),
            P(),
            P(),
        ),
        out_specs=P("scal", "space", None),
        check_vma=False,
    )
```

time: 146 us -> 26.3 us (0.18)
  blocking collectives: 63.4 us -> 0 us
  waiting for transfers between devices: 30.9 us -> 0 us
  Pallas kernels: 0 us -> 21.6 us
  between operations: 18.7 us -> 0.03 us
  starting transfers between devices: 10.8 us -> 0 us
  other arithmetic: 9.39 us -> 0 us
  local copies, waits for them, and re-layouts: 10.2 us -> 4.35 us
  matrix products: 1.83 us -> 0 us
    all_gather x2 -> x0, blocking collectives: 63.4 us -> none  [body(): lax.all_gather(own_slot, 'space', axis=1, tiled=True).astype(jnp.float32)]
    psum x1 -> x0, waiting for transfers between devices: 26.4 us -> none  [from_root(): return lax.psum(kept, axis)]
    pallas_call x0 -> x2, Pallas kernels: none -> 21.6 us  [the longest x1 14 us: body(): pl.pallas_call(functools.partial(gather_kernel, n_space, n_scal), out_sha...]
    ppermute x4 -> x0, starting transfers between devices: 10.8 us -> none  [the longest x2 8.22 us: padded_2(): lax.ppermute(tail, axis, [(i, (i + 1) % count) for i in range(ends)])]
    slice x7 -> x0, local copies, waits for them, and re-layouts: 9.4 us -> none  [the longest x4 6.96 us: advance(): east_cell = jnp.roll(center, -1, axis=2)]
    add x3 -> x0, other arithmetic: 7.74 us -> none  [the longest x2 6.97 us: advance(): center - velocity[0] * (0.5 * (upper_row - lower_row))]
    ppermute x4 -> x0, waiting for transfers between devices: 4.48 us -> none  [the longest x2 4.23 us: padded_2(): lax.ppermute(head, axis, [((i + 1) % count, i) for i in range(ends)])]
    unnamed x6 -> x14, local copies, waits for them, and re-layouts: 0.01 us -> 4.35 us
  transfers between devices with their start and end apart: 5 -> 0, of which waited for: 3 -> 0; matrix products, arithmetic and copies ran while one was open for 8% -> 0% of each run, Pallas kernels for 0% -> 0%
where the time goes in v1:
time: 26.3 us; the launch traced here: 26 us
  Pallas kernels  21.6 us (82%)
  local copies, waits for them, and re-layouts  4.35 us (17%)
    pallas_call x1, Pallas kernels, body(): pl.pallas_call(functools.partial(gather_kernel, n_space, n_scal), out_sha...  14 us
    pallas_call x1, Pallas kernels, body(): pl.pallas_call(functools.partial(stencil_kernel, n_space), out_shape=jax....  7.55 us
    unnamed x14, local copies, waits for them, and re-layouts  4.35 us

profile of v1, /device:TPU:0, one launch (start us, length us, event | category | flops | bytes accessed | tf_op | source)
XLA Modules:
  0.0 26.0 jit_solution(3095450858619725703)
XLA Ops:
  0.0 0.0 copy-start.6
  0.0 0.0 copy-start
  0.0 1.6 %copy-done = f32[32,64,256]{2,1,0:T(8,128)S(1)} copy-done((f32[32,64,256]{2,1,0:T(8,128)S(1)}, f32[32,64,256]{2,1,0:T(8,128)}, u32[]{:S(2)}) %copy-start) | copy-done | bytes 2097176
  1.6 0.0 copy-start.2
  1.6 0.7 %copy-done.2 = bf16[2,2,8,256]{3,2,1,0:T(8,128)(2,1)S(1)} copy-done((bf16[2,2,8,256]{3,2,1,0:T(8,128)(2,1)S(1)}, bf16[2,2,8,256]{3,2,1,0:T(8,128)(2,1)}, u32[]{:S(2)}) %copy-start.2) | copy-done | bytes 16408
  2.3 0.0 copy-start.3
  2.3 0.7 %copy-done.3 = s32[512]{0:T(512)S(1)} copy-done((s32[512]{0:T(512)S(1)}, s32[512]{0:T(512)}, u32[]{:S(2)}) %copy-start.3) | copy-done | bytes 2072
  3.0 0.0 copy-start.4
  3.0 0.7 %copy-done.4 = f32[512]{0:T(512)S(1)} copy-done((f32[512]{0:T(512)S(1)}, f32[512]{0:T(512)}, u32[]{:S(2)}) %copy-start.4) | copy-done | bytes 2072
  3.7 0.0 copy-start.5
  3.7 0.7 %copy-done.5 = s32[2]{0:T(128)S(1)} copy-done((s32[2]{0:T(128)S(1)}, s32[2]{0:T(128)}, u32[]{:S(2)}) %copy-start.5) | copy-done | bytes 32
  4.3 0.0 copy-start.1
  4.3 14.0 %shard_map.64 = (f32[32,8,256]{2,1,0:T(8,128)S(1)}, f32[2,2,72,256]{3,2,1,0:T(8,128)S(1)}) custom-call(s32[2]{0:T(128)S(1)} %copy-done.5, s32[1,512]{1,0:T(1,128)S(1)} %bitcast.2, f32[1,512]{1,0:T(1,128)S(1)} %bitcast.3, bf16[2,2,8,256]{3,2,1,0:T(8,128)(2,1)S(1)} %copy-done.2, f32[32,64,256]{2,1,0:T(8,128)S(1)} %copy-done), custom_call_target="tpu_custom_call" | custom-call | tf_op jit(solution)/shard_map/pallas_call | solution.py:212
  18.4 0.0 copy-done.6
  18.4 0.0 copy-done.1
  18.4 7.6 %shard_map.65 = f32[32,64,256]{2,1,0:T(8,128)} custom-call(f32[32]{0:T(128)S(1)} %copy-done.6, f32[32,8,256]{2,1,0:T(8,128)S(1)} %get-tuple-element.7.halo, f32[2,2,72,256]{3,2,1,0:T(8,128)S(1)} %get-tuple-element.8.vel, f32[32,64,256]{2,1,0:T(8,128)S(1)} %copy-done.1), custom_call_target="tpu_custom_call" | custom-call | tf_op jit(solution)/shard_map/pallas_call | solution.py:236
Async XLA Ops:
  0.0 18.4 %copy-start.6 = (f32[32]{0:T(128)S(1)}, f32[32]{0:T(128)}, u32[]{:S(2)}) copy-start(f32[32]{0:T(128)} %sch.1) | copy-start | bytes 388
  0.0 1.6 %copy-start = (f32[32,64,256]{2,1,0:T(8,128)S(1)}, f32[32,64,256]{2,1,0:T(8,128)}, u32[]{:S(2)}) copy-start(f32[32,64,256]{2,1,0:T(8,128)} %field.3) | copy-start | bytes 6291460
  1.6 0.7 %copy-start.2 = (bf16[2,2,8,256]{3,2,1,0:T(8,128)(2,1)S(1)}, bf16[2,2,8,256]{3,2,1,0:T(8,128)(2,1)}, u32[]{:S(2)}) copy-start(bf16[2,2,8,256]{3,2,1,0:T(8,128)(2,1)} %hist.1) | copy-start | bytes 49156
  2.3 0.7 %copy-start.3 = (s32[512]{0:T(512)S(1)}, s32[512]{0:T(512)}, u32[]{:S(2)}) copy-start(s32[512]{0:T(512)} %param.9) | copy-start | bytes 6148
  3.0 0.7 %copy-start.4 = (f32[512]{0:T(512)S(1)}, f32[512]{0:T(512)}, u32[]{:S(2)}) copy-start(f32[512]{0:T(512)} %param.10) | copy-start | bytes 6148
  3.7 0.7 %copy-start.5 = (s32[2]{0:T(128)S(1)}, s32[2]{0:T(128)}, u32[]{:S(2)}) copy-start(s32[2]{0:T(128)} %snap.1) | copy-start | bytes 28
  4.3 14.1 %copy-start.1 = (f32[32,64,256]{2,1,0:T(8,128)S(1)}, f32[32,64,256]{2,1,0:T(8,128)}, u32[]{:S(2)}) copy-start(f32[32,64,256]{2,1,0:T(8,128)} %field.3) | copy-start | bytes 6291460
